TPU v7x, 256 devices: a whole 4x4x8 slice. The times are simulated.
256 devices in a mesh: dp: 2 (over core), expert: 128 (over z, y, x).
Axes of the slice: x: 4, y: 4, z: 8, core: 2. Of those that a mesh axis runs over, the one named last changes fastest.
Arguments:
- inputs: bfloat16 [8192, 4096], P(('dp', 'expert')), may hold values from -6 to 6
- cotangent: bfloat16 [8192, 4096], P(('dp', 'expert')), may hold values from -6 to 6
- gates: bfloat16 [32768, 2], P(('dp', 'expert')), may hold values from 0.19921875 to 1
- routes: int32 [32768, 2], P(('dp', 'expert')), may hold values from 0 to 127, all different within a row; in each aligned block of 128 rows (0 to 127, 128 to 255, ...) at most 4 rows name the same one
- w_in: bfloat16 [128, 1024, 2048], P('expert', None, 'dp'), may hold values from -0.1875 to 0.1875
- w_out: bfloat16 [128, 2048, 1024], P('expert', 'dp'), may hold values from -0.125 to 0.125
Outputs:
- input_grad: bfloat16 [8192, 4096], P(('dp', 'expert'))
- gate_grad: float32 [32768, 2], P(('dp', 'expert'))
- w_in_grad: bfloat16 [128, 1024, 2048], P('expert', None, 'dp')
- w_out_grad: bfloat16 [128, 2048, 1024], P('expert', 'dp')
Inputs may be any that keep to these rules, and one draw needn't show every extreme that they name: `routes`: within the sub-tokens of one device (aligned blocks of 128 rows), no expert is named more than 4 times, and in every block some expert is named exactly 4 times; the two experts of a row differ.
All inputs are finite; a program needn't handle non-finite values.
Results may differ from a plain program's by a relative error of at most 0.0058.
Values may be sent and summed in bfloat16 or wider, within the bound.
A program may use at most 128 MiB of HBM per device.

v0:
```python
import jax
import jax.numpy as jnp
from jax import lax
from jax.sharding import PartitionSpec as P

HEADS = 4


def gelu_tanh(values):
    inner = 0.7978845608028654 * (values + 0.044715 * values * values * values)
    return 0.5 * values * (1.0 + jnp.tanh(inner))


def gelu_slope(values):
    inner = 0.7978845608028654 * (values + 0.044715 * values * values * values)
    tangent = jnp.tanh(inner)
    return 0.5 * (1.0 + tangent) + 0.5 * values * (1.0 - tangent * tangent) * 0.7978845608028654 * (
        1.0 + 3.0 * 0.044715 * values * values
    )


def expert_terms(rows_in, rows_cot, rows_gate, weight_in, weight_out):
    hidden = jnp.dot(rows_in, weight_in, preferred_element_type=jnp.float32)
    active = gelu_tanh(hidden).astype(jnp.bfloat16)
    output = jnp.dot(active, weight_out, preferred_element_type=jnp.float32)
    dots = jnp.sum(output * rows_cot.astype(jnp.float32), axis=-1)
    scaled = (rows_gate.astype(jnp.float32)[:, None] * rows_cot.astype(jnp.float32)).astype(
        jnp.bfloat16
    )
    back_active = lax.dot_general(
        scaled, weight_out, (((1,), (1,)), ((), ())), preferred_element_type=jnp.float32
    )
    back_hidden = (back_active * gelu_slope(hidden)).astype(jnp.bfloat16)
    grad_out = lax.dot_general(
        active, scaled, (((0,), (0,)), ((), ())), preferred_element_type=jnp.float32
    )
    grad_in = lax.dot_general(
        rows_in, back_hidden, (((0,), (0,)), ((), ())), preferred_element_type=jnp.float32
    )
    row_grads = lax.dot_general(
        back_hidden, weight_in, (((1,), (1,)), ((), ())), preferred_element_type=jnp.float32
    )
    return (grad_in, grad_out, row_grads, dots)


def body(inputs, cotangent, gates, routes, w_in, w_out):
    experts = lax.axis_size("expert")
    local_rows = routes.shape[0]
    width = inputs.shape[1] // HEADS
    capacity = 4 * local_rows // experts
    sub_inputs = inputs.reshape(local_rows, width)
    sub_cot = cotangent.reshape(local_rows, width)
    flat_ids = routes.reshape(-1)
    member = (flat_ids[:, None] == jnp.arange(experts, dtype=jnp.int32)[None, :]).astype(jnp.int32)
    earlier = jnp.cumsum(member, axis=0) - member
    slots = jnp.sum(earlier * member, axis=1)
    target = flat_ids * capacity + slots
    placing = jnp.arange(experts * capacity, dtype=jnp.int32)[:, None] == target[None, :]
    place_pairs = placing.astype(jnp.bfloat16)
    place_rows = jnp.any(placing.reshape(experts * capacity, local_rows, 2), axis=2).astype(
        jnp.bfloat16
    )
    send_in = jnp.dot(place_rows, sub_inputs, preferred_element_type=jnp.float32).astype(
        jnp.bfloat16
    )
    send_cot = jnp.dot(place_rows, sub_cot, preferred_element_type=jnp.float32).astype(jnp.bfloat16)
    send_gate = jnp.dot(place_pairs, gates.reshape(-1), preferred_element_type=jnp.float32).astype(
        jnp.bfloat16
    )
    recv_in, recv_cot, recv_gate = (
        lax.all_to_all(
            send_in.reshape(experts, capacity, width),
            "expert",
            split_axis=0,
            concat_axis=0,
            tiled=True,
        ),
        lax.all_to_all(
            send_cot.reshape(experts, capacity, width),
            "expert",
            split_axis=0,
            concat_axis=0,
            tiled=True,
        ),
        lax.all_to_all(
            send_gate.reshape(experts, capacity), "expert", split_axis=0, concat_axis=0, tiled=True
        ),
    )
    rows_in = recv_in.reshape(experts * capacity, width)
    rows_cot = recv_cot.reshape(experts * capacity, width)
    rows_gate = recv_gate.reshape(experts * capacity)
    full_in, full_out = (
        lax.all_gather(w_in, "dp", axis=2, tiled=True),
        lax.all_gather(w_out, "dp", axis=1, tiled=True),
    )
    grad_in, grad_out, row_grads, dots = expert_terms(
        rows_in, rows_cot, rows_gate, full_in[0], full_out[0]
    )
    summed_in, summed_out = (
        lax.psum_scatter(grad_in[None], "dp", scatter_dimension=2, tiled=True),
        lax.psum_scatter(grad_out[None], "dp", scatter_dimension=1, tiled=True),
    )
    w_in_grad = summed_in.astype(jnp.bfloat16)
    w_out_grad = summed_out.astype(jnp.bfloat16)
    back_grads, back_dots = (
        lax.all_to_all(
            row_grads.reshape(experts, capacity, width),
            "expert",
            split_axis=0,
            concat_axis=0,
            tiled=True,
        ),
        lax.all_to_all(
            dots.reshape(experts, capacity), "expert", split_axis=0, concat_axis=0, tiled=True
        ),
    )
    input_grad = lax.dot_general(
        place_rows.astype(jnp.float32),
        back_grads.reshape(experts * capacity, width),
        (((0,), (0,)), ((), ())),
        precision=lax.Precision.HIGHEST,
        preferred_element_type=jnp.float32,
    )
    gate_grad = lax.dot_general(
        place_pairs.astype(jnp.float32),
        back_dots.reshape(experts * capacity),
        (((0,), (0,)), ((), ())),
        precision=lax.Precision.HIGHEST,
        preferred_element_type=jnp.float32,
    )
    return (
        input_grad.astype(jnp.bfloat16).reshape(inputs.shape),
        gate_grad.reshape(local_rows, 2),
        w_in_grad,
        w_out_grad,
    )


def solution(mesh):
    return jax.shard_map(
        body,
        mesh=mesh,
        in_specs=(
            P(("dp", "expert"), None),
            P(("dp", "expert"), None),
            P(("dp", "expert"), None),
            P(("dp", "expert"), None),
            P("expert", None, "dp"),
            P("expert", "dp", None),
        ),
        out_specs=(
            P(("dp", "expert"), None),
            P(("dp", "expert"), None),
            P("expert", None, "dp"),
            P("expert", "dp", None),
        ),
        check_vma=False,
    )
```

profile of v0, /device:TPU:32, one launch (start us, length us, event | category | flops | bytes accessed | tf_op | source)
XLA Modules:
  0.0 253.8 jit_solution(16300095506976768438)
XLA Ops:
  7.2 0.7 all-gather.5.cloned.1.call-update
  7.9 0.8 copy.44
  9.1 0.2 fusion.26
  9.4 0.8 copy.49
  10.3 0.2 fusion.28
  10.5 0.2 fusion.22
  10.7 0.8 all_to_all.28
  11.5 15.0 %all-to-all-start = ((bf16[128,1,4]{2,1,0:T(2,128)(2,1)}), bf16[128,1,4]{2,1,0:T(2,128)(2,1)S(1)}, u32[]{:S(2)}, u32[]{:S(2)}) async-start(bf16[128,1,4]{2,1,0:T(2,128)(2,1)} %all_to_all.28), calls=%async_computation | async-start | bytes 131072 | tf_op jit(solution)/shard_map/all_to_all | solution.py:85
  26.8 1.2 reshape.131
  28.0 0.4 convolution_convert_fusion.1
  28.5 1.2 reshape.132
  29.7 8.2 %all-to-all-done = bf16[128,1,4]{2,1,0:T(2,128)(2,1)S(1)} async-done(((bf16[128,1,4]{2,1,0:T(2,128)(2,1)}), bf16[128,1,4]{2,1,0:T(2,128)(2,1)S(1)}, u32[]{:S(2)}, u32[]{:S(2)}) %all-to-all-start) | async-done | bytes 1056 | tf_op jit(solution)/shard_map/all_to_all | solution.py:85
  37.9 6.6 %all-to-all-start.1 = ((bf16[128,4,1024]{2,1,0:T(4,128)(2,1)}), bf16[128,4,1024]{2,1,0:T(4,128)(2,1)S(1)}, u32[]{:S(2)}, u32[]{:S(2)}) async-start(bf16[128,4,1024]{2,1,0:T(4,128)(2,1)} %reshape.132), calls=%async_computation.1 | async-start | bytes 2097152 | tf_op jit(solution)/shard_map/all_to_all | solution.py:78
  44.6 0.7 all-gather.3.cloned.1.call-update
  45.5 0.4 convolution_convert_fusion
  45.9 1.2 reshape.134
  47.1 27.6 %all-to-all-done.1 = bf16[128,4,1024]{2,1,0:T(4,128)(2,1)S(1)} async-done(((bf16[128,4,1024]{2,1,0:T(4,128)(2,1)}), bf16[128,4,1024]{2,1,0:T(4,128)(2,1)S(1)}, u32[]{:S(2)}, u32[]{:S(2)}) %all-to-all-start.1) | async-done | bytes 1048608 | tf_op jit(solution)/shard_map/all_to_all | solution.py:78
  74.8 6.1 %all-to-all-start.2 = ((bf16[128,4,1024]{2,1,0:T(4,128)(2,1)}), bf16[128,4,1024]{2,1,0:T(4,128)(2,1)S(1)}, u32[]{:S(2)}, u32[]{:S(2)}) async-start(bf16[128,4,1024]{2,1,0:T(4,128)(2,1)} %reshape.134), calls=%async_computation.2 | async-start | bytes 2097152 | tf_op jit(solution)/shard_map/all_to_all | solution.py:71
  80.8 0.2 reduce-scatter.3.cloned.1.call-start
  81.1 0.5 multiply_convert_fusion.2
  81.6 1.1 convert_element_type.77
  82.7 28.1 %all-to-all-done.2 = bf16[128,4,1024]{2,1,0:T(4,128)(2,1)S(1)} async-done(((bf16[128,4,1024]{2,1,0:T(4,128)(2,1)}), bf16[128,4,1024]{2,1,0:T(4,128)(2,1)S(1)}, u32[]{:S(2)}, u32[]{:S(2)}) %all-to-all-start.2) | async-done | bytes 1048608 | tf_op jit(solution)/shard_map/all_to_all | solution.py:71
  110.9 0.3 reshape.135
  111.2 6.7 %fusion.9 = f32[512,2048]{1,0:T(8,128)} fusion(bf16[512,1024]{1,0:T(8,128)(2,1)S(1)} %reshape.135, bf16[1,1024,2048]{2,1,0:T(8,128)(2,1)} %all-gather.5.cloned.1.call-done), kind=kOutput, calls=%fused_computation.13 | convolution fusion | flops 2147483648 | bytes 9437184 | tf_op jit(solution)/shard_map/dot_general | solution.py:23
  117.8 7.3 %fusion.6 = bf16[512,2048]{1,0:T(8,128)(2,1)S(1)} fusion(f32[512,2048]{1,0:T(8,128)} %fusion.9, bf16[512,1024]{1,0:T(8,128)(2,1)S(1)} %copy-done.1, bf16[1,2048,1024]{2,1,0:T(8,128)(2,1)} %all-gather.3.cloned.1.call-done), kind=kOutput, calls=%fused_computation.10 | convolution fusion | flops 2167406592 | bytes 11534336 | tf_op jit(solution)/shard_map/dot_general | solution.py:30
  125.1 1.3 copy-done
  126.4 5.6 %convolution_bitcast_fusion.1 = f32[1,1024,2048]{2,1,0:T(8,128)} fusion(bf16[512,1024]{1,0:T(8,128)(2,1)S(1)} %reshape.135, bf16[512,2048]{1,0:T(8,128)(2,1)S(1)} %fusion.6), kind=kOutput, calls=%fused_computation.3 | convolution fusion | flops 2147483648 | bytes 11534336 | tf_op jit(solution)/shard_map/dot_general | solution.py:37
  132.1 0.3 reduce-scatter.5.cloned.1.call-start
  132.4 0.2 convert_reduce_fusion
  132.7 0.2 reshape.140
  132.9 9.8 %convolution_bitcast_fusion = f32[1,2048,1024]{2,1,0:T(8,128)} fusion(f32[512,1024]{1,0:T(8,128)S(1)} %reshape.140, f32[512]{0:T(512)S(1)} %reshape.141, f32[512,2048]{1,0:T(8,128)} %fusion.9), kind=kOutput, calls=%fused_computation.2 | convolution fusion | flops 2157969408 | bytes 14682112 | tf_op jit(solution)/shard_map/dot_general | solution.py:34
  142.7 4.4 %dot_general.40 = bf16[128,4,2048]{2,1,0:T(4,128)(2,1)} reshape(bf16[512,2048]{1,0:T(8,128)(2,1)} %copy-done) | data formatting | bytes 4194304 | tf_op jit(solution)/shard_map/dot_general | solution.py:40
  147.0 6.3 %multiply_reduce_fusion = f32[512]{0:T(512)S(1)} fusion(f32[512,1024]{1,0:T(8,128)S(1)} %reshape.140, bf16[1,2048,1024]{2,1,0:T(8,128)(2,1)} %all-gather.3.cloned.1.call-done, f32[512,2048]{1,0:T(8,128)} %fusion.9), kind=kOutput, calls=%fused_computation.22 | convolution fusion | flops 2157968896 | bytes 10487808 | tf_op jit(solution)/shard_map/dot_general | solution.py:25
  153.3 0.7 all_to_all.26
  154.1 6.1 %all-to-all-start.4 = ((f32[128,1,4]{2,1,0:T(1,128)}), f32[128,1,4]{2,1,0:T(1,128)S(1)}, u32[]{:S(2)}, u32[]{:S(2)}) async-start(f32[128,1,4]{2,1,0:T(1,128)} %bitcast.8), calls=%async_computation.4 | async-start | bytes 131072 | tf_op jit(solution)/shard_map/all_to_all | solution.py:113
  160.2 6.6 %fusion.7 = f32[128,4,1024]{2,0,1:T(8,128)S(1)} fusion(bf16[1,1024,2048]{2,1,0:T(8,128)(2,1)} %all-gather.5.cloned.1.call-done, bf16[128,4,2048]{2,1,0:T(4,128)(2,1)} %dot_general.40), kind=kOutput, calls=%fused_computation.11 | convolution fusion | flops 2147483648 | bytes 8388608 | tf_op jit(solution)/shard_map/dot_general | solution.py:40
  166.8 2.7 %copy.52 = f32[128,4,1024]{2,1,0:T(4,128)} copy(f32[128,4,1024]{2,0,1:T(8,128)S(1)} %fusion.7) | data formatting | bytes 4194304 | tf_op jit(solution)/shard_map/dot_general | solution.py:40
  169.5 2.1 all-to-all-done.4
  171.5 11.7 %all-to-all-start.3 = ((f32[128,4,1024]{2,1,0:T(4,128)}), f32[128,4,1024]{2,1,0:T(4,128)S(1)}, u32[]{:S(2)}, u32[]{:S(2)}) async-start(f32[128,4,1024]{2,1,0:T(4,128)} %copy.52), calls=%async_computation.3 | async-start | bytes 4194304 | tf_op jit(solution)/shard_map/all_to_all | solution.py:106
  183.5 0.5 broadcast.81
  184.0 0.8 reduce.7
  185.0 0.9 fusion.23
  185.9 48.7 %all-to-all-done.3 = f32[128,4,1024]{2,1,0:T(4,128)S(1)} async-done(((f32[128,4,1024]{2,1,0:T(4,128)}), f32[128,4,1024]{2,1,0:T(4,128)S(1)}, u32[]{:S(2)}, u32[]{:S(2)}) %all-to-all-start.3) | async-done | bytes 2097184 | tf_op jit(solution)/shard_map/all_to_all | solution.py:106
  234.6 1.7 reshape.136
  236.3 2.5 convolution_convert_fusion.2
  238.8 0.9 reshape.137
  239.6 3.8 %convert_element_type.84 = bf16[1,1024,1024]{2,1,0:T(8,128)(2,1)} convert(f32[1,1024,1024]{2,1,0:T(8,128)} %reduce-scatter.3.cloned.1.call-done) | non-fusion elementwise | flops 1048576 | bytes 6291456 | tf_op jit(solution)/shard_map/convert_element_type | solution.py:103
  243.5 3.8 %convert_element_type.88 = bf16[1,1024,1024]{2,1,0:T(8,128)(2,1)} convert(f32[1,1024,1024]{2,1,0:T(8,128)} %reduce-scatter.5.cloned.1.call-done) | non-fusion elementwise | flops 1048576 | bytes 6291456 | tf_op jit(solution)/shard_map/convert_element_type | solution.py:104
  (37 shorter events, 1.8 us)
Async XLA Ops:
  7.2 20.8 %copy-start.3 = (s32[128,2]{0,1:T(2,128)S(1)}, s32[128,2]{0,1:T(2,128)}, u32[]{:S(2)}) copy-start(s32[128,2]{0,1:T(2,128)} %param.9) | copy-start | bytes 3076
  7.2 104.0 %all-gather.5.cloned.1.call-start = ((), (), s32[]{:S(2)}) async-start(), calls=%async_computation.8 | async-start | bytes 6291456 | tf_op jit(solution)/shard_map/all_gather | solution.py:93
  11.5 26.4 %all-to-all-start = ((bf16[128,1,4]{2,1,0:T(2,128)(2,1)}), bf16[128,1,4]{2,1,0:T(2,128)(2,1)S(1)}, u32[]{:S(2)}, u32[]{:S(2)}) async-start(bf16[128,1,4]{2,1,0:T(2,128)(2,1)} %all_to_all.28), calls=%async_computation | async-start | bytes 131072 | tf_op jit(solution)/shard_map/all_to_all | solution.py:85
  26.5 18.7 %copy-start.2 = (bf16[32,4096]{1,0:T(8,128)(2,1)S(1)}, bf16[32,4096]{1,0:T(8,128)(2,1)}, u32[]{:S(2)}) copy-start(bf16[32,4096]{1,0:T(8,128)(2,1)} %param.6) | copy-start | bytes 786436
  37.9 36.9 %all-to-all-start.1 = ((bf16[128,4,1024]{2,1,0:T(4,128)(2,1)}), bf16[128,4,1024]{2,1,0:T(4,128)(2,1)S(1)}, u32[]{:S(2)}, u32[]{:S(2)}) async-start(bf16[128,4,1024]{2,1,0:T(4,128)(2,1)} %reshape.132), calls=%async_computation.1 | async-start | bytes 2097152 | tf_op jit(solution)/shard_map/all_to_all | solution.py:78
  44.5 73.3 %all-gather.3.cloned.1.call-start = ((), (), s32[]{:S(2)}) async-start(), calls=%async_computation.7 | async-start | bytes 6291456 | tf_op jit(solution)/shard_map/all_gather | solution.py:94
  74.8 36.1 %all-to-all-start.2 = ((bf16[128,4,1024]{2,1,0:T(4,128)(2,1)}), bf16[128,4,1024]{2,1,0:T(4,128)(2,1)S(1)}, u32[]{:S(2)}, u32[]{:S(2)}) async-start(bf16[128,4,1024]{2,1,0:T(4,128)(2,1)} %reshape.134), calls=%async_computation.2 | async-start | bytes 2097152 | tf_op jit(solution)/shard_map/all_to_all | solution.py:71
  80.8 158.8 %reduce-scatter.3.cloned.1.call-start = ((), (), s32[]{:S(2)}) async-start(), calls=%async_computation.9 | async-start | bytes 12582912 | tf_op jit(solution)/shard_map/reduce_scatter | solution.py:100
  111.1 6.7 %copy-start.1 = (bf16[512,1024]{1,0:T(8,128)(2,1)S(1)}, bf16[512,1024]{1,0:T(8,128)(2,1)}, u32[]{:S(2)}) copy-start(bf16[512,1024]{1,0:T(8,128)(2,1)} %convert_element_type.77) | copy-start | bytes 3145732
  125.1 1.3 copy-start
  132.1 111.4 %reduce-scatter.5.cloned.1.call-start = ((), (), s32[]{:S(2)}) async-start(), calls=%async_computation.10 | async-start | bytes 12582912 | tf_op jit(solution)/shard_map/reduce_scatter | solution.py:101
  154.1 17.5 %all-to-all-start.4 = ((f32[128,1,4]{2,1,0:T(1,128)}), f32[128,1,4]{2,1,0:T(1,128)S(1)}, u32[]{:S(2)}, u32[]{:S(2)}) async-start(f32[128,1,4]{2,1,0:T(1,128)} %bitcast.8), calls=%async_computation.4 | async-start | bytes 131072 | tf_op jit(solution)/shard_map/all_to_all | solution.py:113
  171.5 63.0 %all-to-all-start.3 = ((f32[128,4,1024]{2,1,0:T(4,128)}), f32[128,4,1024]{2,1,0:T(4,128)S(1)}, u32[]{:S(2)}, u32[]{:S(2)}) async-start(f32[128,4,1024]{2,1,0:T(4,128)} %copy.52), calls=%async_computation.3 | async-start | bytes 4194304 | tf_op jit(solution)/shard_map/all_to_all | solution.py:106
Sparse Core Ops, SparseCore 0:
  9.8 21.6 all-gather.4
  47.2 20.3 all-gather.2
  132.2 15.7 reduce-scatter.2
  150.6 23.5 reduce-scatter.4
where the time goes:
time: 255 us; the launch traced here: 254 us
  waiting for transfers between devices  116 us (45%)
  matrix products  46.7 us (18%)
  starting transfers between devices  46 us (18%)
  local copies, waits for them, and re-layouts  21 us (8%)
  between operations  14 us (5%)
  other arithmetic  9.88 us (4%)
    all_to_all x1, waiting for transfers between devices, body(): lax.all_to_all(row_grads.reshape(experts, capacity, width), 'expert', spl...  48.7 us
    all_to_all x1, waiting for transfers between devices, body(): lax.all_to_all(send_in.reshape(experts, capacity, width), 'expert', split...  28.1 us
    all_to_all x1, waiting for transfers between devices, body(): lax.all_to_all(send_cot.reshape(experts, capacity, width), 'expert', spli...  27.6 us
    all_to_all x1, starting transfers between devices, body(): lax.all_to_all(send_gate.reshape(experts, capacity), 'expert', split_axis...  15 us
    all_to_all x1, starting transfers between devices, body(): lax.all_to_all(row_grads.reshape(experts, capacity, width), 'expert', spl...  11.7 us
    dot_general x1, matrix products, expert_terms(): lax.dot_general(active, scaled, (((0,), (0,)), ((), ())), preferred_eleme...  9.78 us
    all_to_all x1, waiting for transfers between devices, body(): lax.all_to_all(send_gate.reshape(experts, capacity), 'expert', split_axis...  8.2 us
    dot_general x1, matrix products, expert_terms(): lax.dot_general(scaled, weight_out, (((1,), (1,)), ((), ())), preferred_e...  7.29 us
  transfers between devices with their start and end apart: 9, of which 5 were waited for; matrix products, arithmetic and copies ran while one was open for 23% of the time, Pallas kernels for 0%

commit v1 on v0

v1 whole, which is shorter than its diff:
```python
import functools

import jax
import jax.numpy as jnp
from jax import lax
from jax.experimental import pallas as pl
from jax.experimental.pallas import tpu as pltpu
from jax.sharding import PartitionSpec as P

MESH = pl.DeviceIdType.MESH
F32 = jnp.float32
BF16 = jnp.bfloat16

HEADS = 4
WIDTH = 1024
HID = 1024
TOK = 32
ROWS = 128
NE = 128
CAP = 4
CHUNKS = 4
CH = NE // CHUNKS
GROUP = 16
CROWS = CH * CAP
SIZES = (8, 4, 4)


def offsets(k):
    dz = (k * 5) & 7
    rest = k >> 3
    dx = (rest + dz) & 3
    dy = ((rest >> 2) + (dz >> 1)) & 3
    return dz, dy, dx


def partner(me, k, sign):
    z, y, x = me >> 4, (me >> 2) & 3, me & 3
    dz, dy, dx = offsets(k)
    return (
        ((z + sign * dz + 8) & 7) * 16 + ((y + sign * dy + 4) & 3) * 4 + ((x + sign * dx + 4) & 3)
    )


def iota(shape, axis):
    return lax.broadcasted_iota(jnp.int32, shape, axis)


def dot(a, b, contract=((1,), (0,)), precision=None):
    return lax.dot_general(
        a, b, (contract, ((), ())), precision=precision, preferred_element_type=F32
    )


def kernel(
    routes_ref,
    gates_ref,
    x_ref,
    g_ref,
    win_hbm,
    wout_hbm,
    dx_out,
    gate_out,
    gin_out,
    gout_out,
    win,
    wout,
    table,
    stacked,
    hits,
    send,
    recv,
    recv2,
    back,
    ret,
    dsend,
    dret,
    psend,
    precv,
    pdsend,
    pdrecv,
    xs,
    ss,
    act,
    dhid,
    gin,
    gout,
    gin16,
    gout16,
    acc,
    w_sem,
    send_sem,
    recv_sem,
    fsend_sem,
    frecv_sem,
    bsend_sem,
    brecv_sem,
    dsend_sem,
    drecv_sem,
    psend_sem,
    precv_sem,
    pdsend_sem,
    pdrecv_sem,
    o_sem,
):
    dp = lax.axis_index("dp")
    me = lax.axis_index("expert")
    other = 1 - dp

    barrier = pltpu.get_barrier_semaphore()

    def greet(k, carry):
        pl.semaphore_signal(
            barrier, inc=1, device_id=(dp, partner(me, k, -1)), device_id_type=MESH
        )
        return carry

    lax.fori_loop(1, NE, greet, 0)
    pl.semaphore_signal(barrier, inc=1, device_id=(other, me), device_id_type=MESH)

    load_in = pltpu.make_async_copy(win_hbm, win, w_sem.at[0])
    load_out = pltpu.make_async_copy(wout_hbm, wout, w_sem.at[1])
    load_in.start()
    load_out.start()

    for h in range(HEADS):
        for part in range(2):
            at = h * WIDTH + part * 512
            stacked[pl.ds(part * ROWS + h * TOK, TOK), :] = x_ref[:, at : at + 512]
            stacked[pl.ds((2 + part) * ROWS + h * TOK, TOK), :] = g_ref[:, at : at + 512]
    table[...] = jnp.zeros_like(table)
    table[0:2, :] = routes_ref[...].astype(F32)
    table[2:4, :] = gates_ref[...].astype(F32)
    row, col = iota((ROWS, ROWS), 0), iota((ROWS, ROWS), 1)
    number_of_row, number_of_col = (row & 31) * 4 + (row >> 5), (col & 31) * 4 + (col >> 5)
    reorder = (row == number_of_col).astype(F32).astype(BF16)
    earlier = (number_of_row < number_of_col).astype(F32).astype(BF16)
    own = dot(table[...].astype(BF16), reorder)
    r0, r1, g0, g1 = own[0:1], own[1:2], own[2:3], own[3:4]

    pl.semaphore_wait(barrier, NE)

    def place(j, carry):
        shape = (CH * 16, ROWS)
        line = iota(shape, 0)
        expert = partner(me, j * CH + (line >> 4), 1).astype(F32)
        first, second = expert == r0, expert == r1
        member = jnp.where(first | second, 1.0, 0.0)
        count = dot(member.astype(BF16), earlier)
        slot = (line & 3).astype(F32)
        hit = jnp.where(count == slot, member, 0.0)
        gated = hit * jnp.where(first, g0, g1)
        part = (line >> 2) & 3
        hits[j] = hit.T.astype(BF16)
        spread = jnp.concatenate(
            [
                jnp.where(part == p, hit if p < 2 else gated, 0.0).astype(BF16) for p in range(4)
            ],
            axis=1,
        )
        rows = dot(spread, stacked[...]).astype(BF16)
        send[pl.ds(j * CH, CH)] = rows.reshape(CH, 16, 512)

        @pl.when(j == 0)
        def _():
            pltpu.make_async_copy(send.at[0], recv.at[0], recv_sem.at[0]).start()

        def push(i, c):
            k = j * CH + i
            pltpu.make_async_remote_copy(
                send.at[k],
                recv.at[k],
                send_sem,
                recv_sem.at[j],
                device_id=(dp, partner(me, k, 1)),
                device_id_type=MESH,
            ).start()
            return c

        lax.fori_loop(jnp.where(j == 0, 1, 0), CH, push, 0)
        return carry

    lax.fori_loop(0, CHUNKS, place, 0)

    gin[...] = jnp.zeros_like(gin)
    gout[...] = jnp.zeros_like(gout)
    acc[...] = jnp.zeros_like(acc)
    load_in.wait()
    load_out.wait()

    size = GROUP * 16
    to, frm = iota((size, size), 0), iota((size, size), 1)
    unpack = (
        (frm == ((to & 63) >> 2) * 16 + (to >> 6) * 4 + (to & 3)).astype(F32).astype(BF16)
    )
    pack = (to == ((frm & 63) >> 2) * 16 + (frm >> 6) * 4 + (frm & 3)).astype(F32).astype(BF16)

    def open_rows(source, j, base):
        for b in range(CH // GROUP):
            raw = source[pl.ds(j * CH + b * GROUP, GROUP)].reshape(size, 512)
            rows = dot(unpack, raw).astype(BF16)
            at = base + b * 64
            xs[at : at + 64, 0:512] = rows[0:64]
            xs[at : at + 64, 512:1024] = rows[64:128]
            ss[at : at + 64, 0:512] = rows[128:192]
            ss[at : at + 64, 512:1024] = rows[192:256]

    def step(j, carry):
        mine = pl.ds(j * CH, CH)
        pltpu.make_async_copy(recv.at[mine], recv.at[mine], recv_sem.at[j]).wait()
        forward = pltpu.make_async_remote_copy(
            recv.at[mine],
            recv2.at[mine],
            fsend_sem.at[j],
            frecv_sem.at[j],
            device_id=(other, me),
            device_id_type=MESH,
        )
        forward.start()
        open_rows(recv, j, 0)
        forward.wait_recv()
        open_rows(recv2, j, CROWS)

        dots = jnp.zeros((2 * CROWS, 1), F32)
        for b in range(HID // 256):
            cols = slice(b * 256, b * 256 + 256)
            hidden = dot(xs[...], win[:, cols])
            pulled = dot(ss[...], wout[cols, :], ((1,), (1,)))
            square = hidden * hidden
            tangent = jnp.tanh(0.7978845608028654 * (hidden + 0.044715 * square * hidden))
            active = (0.5 * hidden * (1.0 + tangent)).astype(BF16)
            slope = 0.5 * (1.0 + tangent) + 0.5 * hidden * (
                1.0 - tangent * tangent
            ) * 0.7978845608028654 * (1.0 + 3.0 * 0.044715 * square)
            act[:, cols] = active
            dhid[:, cols] = (pulled * slope).astype(BF16)
            dots = dots + jnp.sum(active.astype(F32) * pulled, axis=1, keepdims=True)
        partial = dot(dhid[...], win[...], ((1,), (1,)))
        psend[j] = partial[CROWS:].astype(BF16)
        wide = jnp.broadcast_to(dots, (2 * CROWS, 128))
        pdsend[j] = wide[CROWS:]
        swap = pltpu.make_async_remote_copy(
            psend.at[j],
            precv.at[j],
            psend_sem.at[j],
            precv_sem.at[j],
            device_id=(other, me),
            device_id_type=MESH,
        )
        swap_dots = pltpu.make_async_remote_copy(
            pdsend.at[j],
            pdrecv.at[j],
            pdsend_sem.at[j],
            pdrecv_sem.at[j],
            device_id=(other, me),
            device_id_type=MESH,
        )
        swap.start()
        swap_dots.start()
        for b in range(HID // 256):
            cols = slice(b * 256, b * 256 + 256)
            gout[cols, :] += dot(act[:, cols], ss[...], ((0,), (0,)))
            gin[cols, :] += dot(xs[:, cols], dhid[...], ((0,), (0,)))
        swap.wait_recv()
        swap_dots.wait_recv()
        whole = (partial[:CROWS] + precv[j].astype(F32)).astype(BF16)
        for b in range(CH // GROUP):
            rows = whole[b * 64 : b * 64 + 64]
            tall = jnp.concatenate([rows[:, p * 256 : p * 256 + 256] for p in range(4)], axis=0)
            back[pl.ds(j * CH + b * GROUP, GROUP)] = (
                dot(pack, tall).astype(BF16).reshape(GROUP, 16, 256)
            )
        all_dots = wide[:CROWS] + pdrecv[j]
        line, lane = iota((CROWS, 128), 0), iota((CROWS, 128), 1)
        spread = jnp.where((line & 3) == lane, all_dots, 0.0)
        gather = (iota((CH, CROWS), 0) == (iota((CH, CROWS), 1) >> 2)).astype(F32)
        dsend[mine] = dot(gather, spread, precision=lax.Precision.HIGHEST).reshape(CH, 1, 128)

        @pl.when(j == 0)
        def _():
            pltpu.make_async_copy(back.at[0], ret.at[0], brecv_sem.at[0]).start()
            pltpu.make_async_copy(dsend.at[0], dret.at[0], drecv_sem.at[0]).start()

        def push(i, c):
            k = j * CH + i
            target = (dp, partner(me, k, -1))
            pltpu.make_async_remote_copy(
                back.at[k],
                ret.at[k],
                bsend_sem,
                brecv_sem.at[j],
                device_id=target,
                device_id_type=MESH,
            ).start()
            pltpu.make_async_remote_copy(
                dsend.at[k],
                dret.at[k],
                dsend_sem,
                drecv_sem.at[j],
                device_id=target,
                device_id_type=MESH,
            ).start()
            return c

        lax.fori_loop(jnp.where(j == 0, 1, 0), CH, push, 0)
        return carry

    lax.fori_loop(0, CHUNKS, step, 0)

    gin16[...] = gin[...].astype(BF16)
    gout16[...] = gout[...].astype(BF16)
    store_in = pltpu.make_async_copy(gin16, gin_out, o_sem.at[0])
    store_out = pltpu.make_async_copy(gout16, gout_out, o_sem.at[1])
    store_in.start()
    store_out.start()

    def collect(j, carry):
        mine = pl.ds(j * CH, CH)
        pltpu.make_async_copy(ret.at[mine], ret.at[mine], brecv_sem.at[j]).wait()
        lane = iota((ROWS, CH * 16), 1)
        hit = hits[j].astype(F32)
        picks = jnp.concatenate(
            [jnp.where(((lane >> 2) & 3) == q, hit, 0.0).astype(BF16) for q in range(4)], axis=0
        )
        acc[...] += dot(picks, ret[mine].reshape(CH * 16, 256))
        return carry

    lax.fori_loop(0, CHUNKS, collect, 0)
    for h in range(HEADS):
        for q in range(4):
            at = h * WIDTH + q * 256
            dx_out[:, at : at + 256] = acc[
                q * ROWS + h * TOK : q * ROWS + h * TOK + TOK, :
            ].astype(BF16)

    for j in range(CHUNKS):
        mine = pl.ds(j * CH, CH)
        pltpu.make_async_copy(dret.at[mine], dret.at[mine], drecv_sem.at[j]).wait()
    values = dret[...].reshape(NE, 128)
    expert = partner(me, iota((NE, ROWS), 0), 1).astype(F32)
    n0, n1 = table[0:1], table[1:2]
    first, second = expert == n0, expert == n1
    member = jnp.where(first | second, 1.0, 0.0)
    before = (row < col).astype(F32).astype(BF16)
    count = dot(member.astype(BF16), before)
    picked = jnp.zeros((NE, ROWS), F32)
    for s in range(CAP):
        picked = picked + jnp.where(count == float(s), values[:, s : s + 1], 0.0)
    gate_out[0:1, :] = (
        jnp.sum(jnp.where(first, picked, 0.0), axis=0, keepdims=True) / table[2:3]
    )
    gate_out[1:2, :] = (
        jnp.sum(jnp.where(second, picked, 0.0), axis=0, keepdims=True) / table[3:4]
    )

    rest = pl.ds(1, NE - 1)
    pltpu.make_async_copy(send.at[rest], send.at[rest], send_sem).wait()
    pltpu.make_async_copy(back.at[rest], back.at[rest], bsend_sem).wait()
    pltpu.make_async_copy(dsend.at[rest], dsend.at[rest], dsend_sem).wait()
    for j in range(CHUNKS):
        mine = pl.ds(j * CH, CH)
        pltpu.make_async_copy(recv.at[mine], recv.at[mine], fsend_sem.at[j]).wait()
        pltpu.make_async_copy(psend.at[j], psend.at[j], psend_sem.at[j]).wait()
        pltpu.make_async_copy(pdsend.at[j], pdsend.at[j], pdsend_sem.at[j]).wait()
    store_in.wait()
    store_out.wait()


def body(inputs, cotangent, gates, routes, w_in, w_out):
    vmem, hbm = pl.BlockSpec(memory_space=pltpu.VMEM), pl.BlockSpec(memory_space=pl.ANY)
    dma = pltpu.SemaphoreType.DMA
    dx, gate, gin, gout = pl.pallas_call(
        kernel,
        out_shape=(
            jax.ShapeDtypeStruct(inputs.shape, BF16),
            jax.ShapeDtypeStruct((2, ROWS), F32),
            jax.ShapeDtypeStruct((WIDTH, HID), BF16),
            jax.ShapeDtypeStruct((HID, WIDTH), BF16),
        ),
        in_specs=[vmem, vmem, vmem, vmem, hbm, hbm],
        out_specs=(vmem, vmem, hbm, hbm),
        scratch_shapes=[
            pltpu.VMEM((WIDTH, HID), BF16),
            pltpu.VMEM((HID, WIDTH), BF16),
            pltpu.VMEM((8, ROWS), F32),
            pltpu.VMEM((4 * ROWS, 512), BF16),
            pltpu.VMEM((CHUNKS, ROWS, CH * 16), BF16),
            pltpu.VMEM((NE, 16, 512), BF16),
            pltpu.VMEM((NE, 16, 512), BF16),
            pltpu.VMEM((NE, 16, 512), BF16),
            pltpu.VMEM((NE, 16, 256), BF16),
            pltpu.VMEM((NE, 16, 256), BF16),
            pltpu.VMEM((NE, 1, 128), F32),
            pltpu.VMEM((NE, 1, 128), F32),
            pltpu.VMEM((CHUNKS, CROWS, WIDTH), BF16),
            pltpu.VMEM((CHUNKS, CROWS, WIDTH), BF16),
            pltpu.VMEM((CHUNKS, CROWS, 128), F32),
            pltpu.VMEM((CHUNKS, CROWS, 128), F32),
            pltpu.VMEM((2 * CROWS, WIDTH), BF16),
            pltpu.VMEM((2 * CROWS, WIDTH), BF16),
            pltpu.VMEM((2 * CROWS, HID), BF16),
            pltpu.VMEM((2 * CROWS, HID), BF16),
            pltpu.VMEM((WIDTH, HID), F32),
            pltpu.VMEM((HID, WIDTH), F32),
            pltpu.VMEM((WIDTH, HID), BF16),
            pltpu.VMEM((HID, WIDTH), BF16),
            pltpu.VMEM((4 * ROWS, 256), F32),
            dma((2,)),
            dma,
            dma((CHUNKS,)),
            dma((CHUNKS,)),
            dma((CHUNKS,)),
            dma,
            dma((CHUNKS,)),
            dma,
            dma((CHUNKS,)),
            dma((CHUNKS,)),
            dma((CHUNKS,)),
            dma((CHUNKS,)),
            dma((CHUNKS,)),
            dma((2,)),
        ],
        compiler_params=pltpu.CompilerParams(
            collective_id=0, has_side_effects=True, vmem_limit_bytes=56 << 20
        ),
        name="experts",
    )(routes.T, gates.T, inputs, cotangent, w_in[0], w_out[0])
    return dx, gate.T, gin[None], gout[None]


def solution(mesh):
    return jax.shard_map(
        body,
        mesh=mesh,
        in_specs=(
            P(("dp", "expert"), None),
            P(("dp", "expert"), None),
            P(("dp", "expert"), None),
            P(("dp", "expert"), None),
            P("expert", None, "dp"),
            P("expert", "dp", None),
        ),
        out_specs=(
            P(("dp", "expert"), None),
            P(("dp", "expert"), None),
            P("expert", None, "dp"),
            P("expert", "dp", None),
        ),
        check_vma=False,
    )
```

time: 255 us -> 96.9 us (0.38)
  the two profiles are of different devices: /device:TPU:32 before, /device:TPU:1 now
where the time goes in v1:
time: 96.9 us; the launch traced here: 96.8 us
  Pallas kernels  88.7 us (92%)
  local copies, waits for them, and re-layouts  7.42 us (8%)
    pallas_call x1, Pallas kernels, body(): pl.pallas_call(kernel, out_shape=(jax.ShapeDtypeStruct(inputs.shape, BF16...  88.7 us
    unnamed x6, local copies, waits for them, and re-layouts  7.42 us

profile of v1, /device:TPU:1, one launch (start us, length us, event | category | flops | bytes accessed | tf_op | source)
XLA Modules:
  0.0 96.8 jit_solution(16612378167730196032)
XLA Ops:
  0.6 88.7 %experts.1 = (bf16[32,4096]{1,0:T(8,128)(2,1)}, f32[2,128]{1,0:T(2,128)}, bf16[1024,1024]{1,0:T(8,128)(2,1)}, bf16[1024,1024]{1,0:T(8,128)(2,1)}) custom-call(s32[2,128]{1,0:T(2,128)} %bitcast.12, bf16[2,128]{1,0:T(2,128)(2,1)} %bitcast.13, bf16[32,4096]{1,0:T(8,128)(2,1)} %x_ref.1, bf16[32,4096]{1,0:T(8,128)(2,1)} %g_ref.1, bf16[1024,1024]{1,0:T(8,128)(2,1)} %bitcast.7, ...), custom_call_target="tpu_custom_call" | custom-call | tf_op jit(solution)/shard_map/experts/pallas_call | solution.py:371
  89.3 1.7 %copy.14 = bf16[32,4096]{1,0:T(8,128)(2,1)} copy(bf16[32,4096]{1,0:T(8,128)(2,1)} %get-tuple-element.16) | data formatting | bytes 524288
  91.0 1.2 %copy.15 = f32[128,2]{0,1:T(2,128)} copy(f32[128,2]{0,1:T(2,128)} %bitcast.11) | data formatting | bytes 2048
  92.2 0.0 copy-start
  92.2 3.2 %copy.16 = bf16[1,1024,1024]{2,1,0:T(8,128)(2,1)} copy(bf16[1,1024,1024]{2,1,0:T(8,128)(2,1)} %bitcast.10) | data formatting | bytes 4194304
  95.5 0.0 copy-done
  95.5 1.3 %copy.17 = bf16[1,1024,1024]{2,1,0:T(8,128)(2,1)} copy(bf16[1,1024,1024]{2,1,0:T(8,128)(2,1)S(1)} %bitcast.9) | data formatting | bytes 4194304
Async XLA Ops:
  92.2 3.2 %copy-start = (bf16[1024,1024]{1,0:T(8,128)(2,1)S(1)}, bf16[1024,1024]{1,0:T(8,128)(2,1)}, u32[]{:S(2)}) copy-start(bf16[1024,1024]{1,0:T(8,128)(2,1)} %get-tuple-element.11) | copy-start | bytes 6291460

commit v2 on v1

v2 whole, which is shorter than its diff:
```python
import functools

import jax
import jax.numpy as jnp
from jax import lax
from jax.experimental import pallas as pl
from jax.experimental.pallas import tpu as pltpu
from jax.sharding import PartitionSpec as P

MESH = pl.DeviceIdType.MESH
F32 = jnp.float32
BF16 = jnp.bfloat16

HEADS = 4
WIDTH = 1024
HID = 1024
TOK = 32
ROWS = 128
NE = 128
CAP = 4
CHUNKS = 4
CH = NE // CHUNKS
GROUP = 16
CROWS = CH * CAP
SIZES = (8, 4, 4)


def offsets(k):
    plane, place = k >> 4, k & 15
    dz = (4 - (plane >> 1)) * (1 - 2 * (plane & 1)) + 4 * (1 - ((plane + 7) >> 3))
    return dz, place >> 2, place & 3


def partner(me, k, sign, lift=0):
    z, y, x = me >> 4, (me >> 2) & 3, me & 3
    dz, dy, dx = offsets(k)
    return (
        ((z + sign * dz + lift + 16) & 7) * 16
        + ((y + sign * dy + 4) & 3) * 4
        + ((x + sign * dx + 4) & 3)
    )


def iota(shape, axis):
    return lax.broadcasted_iota(jnp.int32, shape, axis)


def dot(a, b, contract=((1,), (0,)), precision=None):
    return lax.dot_general(
        a, b, (contract, ((), ())), precision=precision, preferred_element_type=F32
    )


def kernel(
    routes_hbm,
    gates_hbm,
    x_hbm,
    g_hbm,
    win_hbm,
    wout_hbm,
    dx_out,
    gate_out,
    gin_out,
    gout_out,
    win,
    wout,
    routes_ref,
    gates_ref,
    x_ref,
    g_ref,
    raw_table,
    table,
    stack_x,
    stack_g,
    near_table,
    near_x,
    near_g,
    near_stack_x,
    near_stack_g,
    hits,
    plan_x,
    plan_s,
    send_x,
    send_s,
    recv_x,
    recv_s,
    recv2_x,
    recv2_s,
    back,
    ret,
    dsend,
    dret,
    psend,
    precv,
    pdsend,
    pdrecv,
    xs,
    ss,
    act,
    dhid,
    gin,
    gout,
    acc,
    w_sem,
    line_sem,
    t_send,
    t_recv,
    send_sem,
    rx_sem,
    rs_sem,
    fsend_sem,
    fx_sem,
    fs_sem,
    bsend_sem,
    brecv_sem,
    dsend_sem,
    drecv_sem,
    psend_sem,
    precv_sem,
    pdsend_sem,
    pdrecv_sem,
):
    dp = lax.axis_index("dp")
    me = lax.axis_index("expert")
    other = 1 - dp
    loads = [
        pltpu.make_async_copy(source, target, w_sem.at[2 + n])
        for n, (source, target) in enumerate(
            ((routes_hbm, routes_ref), (gates_hbm, gates_ref), (x_hbm, x_ref), (g_hbm, g_ref))
        )
    ]
    for load in loads:
        load.start()

    barrier = pltpu.get_barrier_semaphore()

    def along(axis, step):
        z, y, x = me >> 4, (me >> 2) & 3, me & 3
        if axis == 0:
            z = (z + step) & 7
        elif axis == 1:
            y = (y + step) & 3
        else:
            x = (x + step) & 3
        return (dp, z * 16 + y * 4 + x)

    def greet(semaphore, axis):
        for step in (1, 7, 2, 6, 3, 5, 4) if axis == 0 else (1, 3, 2):
            pl.semaphore_signal(
                semaphore, inc=1, device_id=along(axis, step), device_id_type=MESH
            )

    for axis in range(3):
        greet(barrier, axis)
    pl.semaphore_signal(barrier, inc=1, device_id=(other, me), device_id_type=MESH)
    pl.semaphore_wait(barrier, 14)

    def hand(n, source, target):
        copies = []
        for side in range(2):
            copy = pltpu.make_async_remote_copy(
                source,
                target.at[side],
                t_send.at[n, side],
                t_recv.at[n, side],
                device_id=along(0, 1 - 2 * side),
                device_id_type=MESH,
            )
            copy.start()
            copies.append(copy)
        return copies

    hand_x = hand(1, x_hbm, near_x)
    greet(line_sem.at[0], 1)

    row, col = iota((ROWS, ROWS), 0), iota((ROWS, ROWS), 1)
    number_of_row, number_of_col = (row & 31) * 4 + (row >> 5), (col & 31) * 4 + (col >> 5)
    reorder = (row == number_of_col).astype(F32).astype(BF16)
    earlier = (number_of_row < number_of_col).astype(F32).astype(BF16)
    raw_table[...] = jnp.zeros_like(raw_table)
    loads[0].wait()
    loads[1].wait()
    raw_table[0:2, :] = routes_ref[...].astype(F32)
    raw_table[2:4, :] = gates_ref[...].astype(F32)
    table[...] = dot(raw_table[...].astype(BF16), reorder)
    hand_table = hand(0, table, near_table)
    hand_g = hand(2, g_hbm, near_g)

    def stack(source, target):
        for h in range(HEADS):
            for part in range(4):
                at = h * WIDTH + part * 256
                target[pl.ds(part * ROWS + h * TOK, TOK), :] = source[:, at : at + 256]

    pl.semaphore_wait(line_sem.at[0], 3)
    greet(line_sem.at[1], 2)

    def chosen(source, lines, first_line, origin, base):
        shape = (lines, ROWS)
        line = iota(shape, 0) + first_line
        expert = partner(origin, base + (line >> 4), 1).astype(F32)
        first, second = expert == source[0:1], expert == source[1:2]
        member = jnp.where(first | second, 1.0, 0.0)
        count = dot(member.astype(BF16), earlier)
        hit = jnp.where(count == (line & 3).astype(F32), member, 0.0)
        return line, first, hit

    def plan(unit, source, lines, first_line, origin, base):
        line, first, hit = chosen(source, lines, first_line, origin, base)
        gated = hit * jnp.where(first, source[2:3], source[3:4])
        part = (line >> 2) & 3
        at = pl.ds(first_line, lines)
        for p in range(4):
            cols = slice(p * ROWS, p * ROWS + ROWS)
            plan_x[unit, at, cols] = jnp.where(part == p, hit, 0.0).astype(BF16)
            plan_s[unit, at, cols] = jnp.where(part == p, gated, 0.0).astype(BF16)

    def place(unit, plans, stacks, sends, recvs, sems, side):
        base, start, stop = unit * 16, 0, 16
        if unit == 1:
            start, stop = side * 8, side * 8 + 8
        tokens = stacks if side is None else stacks.at[side]
        lines = slice(start * 16, stop * 16)
        made = dot(plans[unit, lines, :], tokens[...]).astype(BF16)
        sends[base + start : base + stop] = made.reshape(stop - start, 16, 256)
        lift = 0 if side is None else (-1, 1)[side]
        sem = sems.at[unit // 2]
        if unit in (0, 6, 7):
            pltpu.make_async_copy(sends.at[base], recvs.at[base], sem).start()
            start = 1

        def push(i, carry):
            k = base + i
            pltpu.make_async_remote_copy(
                sends.at[k],
                recvs.at[k],
                send_sem,
                sem,
                device_id=(dp, partner(me, k, 1, lift)),
                device_id_type=MESH,
            ).start()
            return carry

        lax.fori_loop(start, stop, push, 0)

    plan(0, table[...], 256, 0, me, 0)
    loads[2].wait()
    loads[3].wait()
    stack(x_ref, stack_x)
    stack(g_ref, stack_g)
    pl.semaphore_wait(line_sem.at[1], 3)
    place(0, plan_x, stack_x, send_x, recv_x, rx_sem, None)
    place(0, plan_s, stack_g, send_s, recv_s, rs_sem, None)
    for side in range(2):
        hand_table[side].wait_recv()
    origins = (along(0, -1)[1], along(0, 1)[1])
    units = ((1, 0), (1, 1), (2, 0), (3, 1), (6, 0), (7, 1), (4, 0), (5, 1))
    for unit, side in units:
        lines, first_line = (128, 128 * side) if unit == 1 else (256, 0)
        plan(unit, near_table[side], lines, first_line, origins[side], unit * 16)
    for side in range(2):
        hand_x[side].wait_recv()
        stack(near_x.at[side], near_stack_x.at[side])
    for unit, side in units:
        place(unit, plan_x, near_stack_x, send_x, recv_x, rx_sem, side)
    for side in range(2):
        hand_g[side].wait_recv()
        stack(near_g.at[side], near_stack_g.at[side])
    for unit, side in units:
        place(unit, plan_s, near_stack_g, send_s, recv_s, rs_sem, side)

    load_in = pltpu.make_async_copy(win_hbm, win, w_sem.at[0])
    load_out = pltpu.make_async_copy(wout_hbm, wout, w_sem.at[1])
    load_in.start()
    load_out.start()

    def remember(j, carry):
        _, _, hit = chosen(table[...], CH * 16, 0, me, j * CH)
        hits[j] = hit.T.astype(BF16)
        return carry

    lax.fori_loop(0, CHUNKS, remember, 0)
    gin[...] = jnp.zeros_like(gin)
    gout[...] = jnp.zeros_like(gout)
    acc[...] = jnp.zeros_like(acc)
    load_in.wait()
    load_out.wait()

    size = GROUP * 16
    to, frm = iota((size, size), 0), iota((size, size), 1)
    unpack = (
        (frm == ((to & 63) >> 2) * 16 + (to >> 6) * 4 + (to & 3)).astype(F32).astype(BF16)
    )
    pack = (to == ((frm & 63) >> 2) * 16 + (frm >> 6) * 4 + (frm & 3)).astype(F32).astype(BF16)

    def open_rows(source, target, j, base):
        for b in range(CH // GROUP):
            raw = source[pl.ds(j * CH + b * GROUP, GROUP)].reshape(size, 256)
            rows = dot(unpack, raw).astype(BF16)
            at = base + b * 64
            for p in range(4):
                target[at : at + 64, p * 256 : p * 256 + 256] = rows[p * 64 : p * 64 + 64]

    def step(j, carry):
        mine = pl.ds(j * CH, CH)
        forwards = []
        for n, (got, passed, sem, fsem) in enumerate(
            ((recv_x, recv2_x, rx_sem, fx_sem), (recv_s, recv2_s, rs_sem, fs_sem))
        ):
            pltpu.make_async_copy(got.at[mine], got.at[mine], sem.at[j]).wait()
            forward = pltpu.make_async_remote_copy(
                got.at[mine],
                passed.at[mine],
                fsend_sem.at[n, j],
                fsem.at[j],
                device_id=(other, me),
                device_id_type=MESH,
            )
            forward.start()
            forwards.append(forward)
            open_rows(got, (xs, ss)[n], j, 0)
        forwards[0].wait_recv()
        open_rows(recv2_x, xs, j, CROWS)
        forwards[1].wait_recv()
        open_rows(recv2_s, ss, j, CROWS)

        dots = jnp.zeros((2 * CROWS, 1), F32)
        for b in range(HID // 256):
            cols = slice(b * 256, b * 256 + 256)
            hidden = dot(xs[...], win[:, cols])
            pulled = dot(ss[...], wout[cols, :], ((1,), (1,)))
            square = hidden * hidden
            tangent = jnp.tanh(0.7978845608028654 * (hidden + 0.044715 * square * hidden))
            active = (0.5 * hidden * (1.0 + tangent)).astype(BF16)
            slope = 0.5 * (1.0 + tangent) + 0.5 * hidden * (
                1.0 - tangent * tangent
            ) * 0.7978845608028654 * (1.0 + 3.0 * 0.044715 * square)
            act[:, cols] = active
            dhid[:, cols] = (pulled * slope).astype(BF16)
            dots = dots + jnp.sum(active.astype(F32) * pulled, axis=1, keepdims=True)
        partial = dot(dhid[...], win[...], ((1,), (1,)))
        psend[j] = partial[CROWS:].astype(BF16)
        wide = jnp.broadcast_to(dots, (2 * CROWS, 128))
        pdsend[j] = wide[CROWS:]
        swap = pltpu.make_async_remote_copy(
            psend.at[j],
            precv.at[j],
            psend_sem.at[j],
            precv_sem.at[j],
            device_id=(other, me),
            device_id_type=MESH,
        )
        swap_dots = pltpu.make_async_remote_copy(
            pdsend.at[j],
            pdrecv.at[j],
            pdsend_sem.at[j],
            pdrecv_sem.at[j],
            device_id=(other, me),
            device_id_type=MESH,
        )
        swap.start()
        swap_dots.start()
        for b in range(HID // 256):
            cols = slice(b * 256, b * 256 + 256)
            gout[cols, :] += dot(act[:, cols], ss[...], ((0,), (0,)))
            gin[cols, :] += dot(xs[:, cols], dhid[...], ((0,), (0,)))
        swap.wait_recv()
        swap_dots.wait_recv()
        whole = (partial[:CROWS] + precv[j].astype(F32)).astype(BF16)
        for b in range(CH // GROUP):
            rows = whole[b * 64 : b * 64 + 64]
            tall = jnp.concatenate([rows[:, p * 256 : p * 256 + 256] for p in range(4)], axis=0)
            back[pl.ds(j * CH + b * GROUP, GROUP)] = (
                dot(pack, tall).astype(BF16).reshape(GROUP, 16, 256)
            )
        all_dots = wide[:CROWS] + pdrecv[j]
        line, lane = iota((CROWS, 128), 0), iota((CROWS, 128), 1)
        spread = jnp.where((line & 3) == lane, all_dots, 0.0)
        gather = (iota((CH, CROWS), 0) == (iota((CH, CROWS), 1) >> 2)).astype(F32)
        dsend[mine] = dot(gather, spread, precision=lax.Precision.HIGHEST).reshape(CH, 1, 128)

        @pl.when(j == 0)
        def _():
            pltpu.make_async_copy(back.at[0], ret.at[0], brecv_sem.at[0]).start()
            pltpu.make_async_copy(dsend.at[0], dret.at[0], drecv_sem.at[0]).start()

        def push(i, c):
            k = j * CH + i
            target = (dp, partner(me, k, -1))
            pltpu.make_async_remote_copy(
                back.at[k],
                ret.at[k],
                bsend_sem,
                brecv_sem.at[j],
                device_id=target,
                device_id_type=MESH,
            ).start()
            pltpu.make_async_remote_copy(
                dsend.at[k],
                dret.at[k],
                dsend_sem,
                drecv_sem.at[j],
                device_id=target,
                device_id_type=MESH,
            ).start()
            return c

        lax.fori_loop(jnp.where(j == 0, 1, 0), CH, push, 0)
        return carry

    lax.fori_loop(0, CHUNKS, step, 0)

    gin_out[...] = gin[...].astype(BF16)
    gout_out[...] = gout[...].astype(BF16)

    expert = partner(me, iota((NE, ROWS), 0), 1).astype(F32)
    n0, n1 = raw_table[0:1], raw_table[1:2]
    first, second = expert == n0, expert == n1
    member = jnp.where(first | second, 1.0, 0.0)
    before = (row < col).astype(F32).astype(BF16)
    count = dot(member.astype(BF16), before)

    def collect(j, carry):
        mine = pl.ds(j * CH, CH)
        lane = iota((ROWS, CH * 16), 1)
        hit = hits[j].astype(F32)
        picks = jnp.concatenate(
            [jnp.where(((lane >> 2) & 3) == q, hit, 0.0).astype(BF16) for q in range(4)], axis=0
        )
        pltpu.make_async_copy(ret.at[mine], ret.at[mine], brecv_sem.at[j]).wait()
        acc[...] += dot(picks, ret[mine].reshape(CH * 16, 256))
        return carry

    lax.fori_loop(0, CHUNKS, collect, 0)
    for h in range(HEADS):
        for q in range(4):
            at = h * WIDTH + q * 256
            dx_out[:, at : at + 256] = acc[
                q * ROWS + h * TOK : q * ROWS + h * TOK + TOK, :
            ].astype(BF16)

    for j in range(CHUNKS):
        mine = pl.ds(j * CH, CH)
        pltpu.make_async_copy(dret.at[mine], dret.at[mine], drecv_sem.at[j]).wait()
    values = dret[...].reshape(NE, 128)
    picked = jnp.zeros((NE, ROWS), F32)
    for s in range(CAP):
        picked = picked + jnp.where(count == float(s), values[:, s : s + 1], 0.0)
    gate_out[0:1, :] = (
        jnp.sum(jnp.where(first, picked, 0.0), axis=0, keepdims=True) / raw_table[2:3]
    )
    gate_out[1:2, :] = (
        jnp.sum(jnp.where(second, picked, 0.0), axis=0, keepdims=True) / raw_table[3:4]
    )

    rest = pl.ds(1, NE - 1)
    for copy in hand_table + hand_x + hand_g:
        copy.wait_send()
    sent = pl.ds(3, NE - 3)
    pltpu.make_async_copy(send_x.at[sent], send_x.at[sent], send_sem).wait()
    pltpu.make_async_copy(send_s.at[sent], send_s.at[sent], send_sem).wait()
    pltpu.make_async_copy(back.at[rest], back.at[rest], bsend_sem).wait()
    pltpu.make_async_copy(dsend.at[rest], dsend.at[rest], dsend_sem).wait()
    for j in range(CHUNKS):
        mine = pl.ds(j * CH, CH)
        pltpu.make_async_copy(recv_x.at[mine], recv_x.at[mine], fsend_sem.at[0, j]).wait()
        pltpu.make_async_copy(recv_s.at[mine], recv_s.at[mine], fsend_sem.at[1, j]).wait()
        pltpu.make_async_copy(psend.at[j], psend.at[j], psend_sem.at[j]).wait()
        pltpu.make_async_copy(pdsend.at[j], pdsend.at[j], pdsend_sem.at[j]).wait()


def flush(dx, gate, gin, gout, dx_out, gate_out, gin_out, gout_out, sems):
    copies = [
        pltpu.make_async_copy(source, target, sems.at[n])
        for n, (source, target) in enumerate(
            ((gin, gin_out), (gout, gout_out), (dx, dx_out), (gate, gate_out))
        )
    ]
    for copy in copies:
        copy.start()
    for copy in copies:
        copy.wait()


def body(inputs, cotangent, gates, routes, w_in, w_out):
    vmem, hbm = pl.BlockSpec(memory_space=pltpu.VMEM), pl.BlockSpec(memory_space=pl.ANY)
    dma = pltpu.SemaphoreType.DMA
    shapes = (
        (inputs.shape, BF16),
        ((2, ROWS), F32),
        ((WIDTH, HID), BF16),
        ((HID, WIDTH), BF16),
    )
    outs = pl.pallas_call(
        kernel,
        out_shape=tuple(pltpu.VMEM(shape, kind) for shape, kind in shapes),
        in_specs=[hbm] * 6,
        out_specs=(vmem,) * 4,
        scratch_shapes=[
            pltpu.VMEM((WIDTH, HID), BF16),
            pltpu.VMEM((HID, WIDTH), BF16),
            pltpu.VMEM(routes.shape[::-1], jnp.int32),
            pltpu.VMEM(gates.shape[::-1], BF16),
            pltpu.VMEM(inputs.shape, BF16),
            pltpu.VMEM(inputs.shape, BF16),
            pltpu.VMEM((8, ROWS), F32),
            pltpu.VMEM((8, ROWS), F32),
            pltpu.VMEM((4 * ROWS, 256), BF16),
            pltpu.VMEM((4 * ROWS, 256), BF16),
            pltpu.VMEM((2, 8, ROWS), F32),
            pltpu.VMEM((2,) + inputs.shape, BF16),
            pltpu.VMEM((2,) + inputs.shape, BF16),
            pltpu.VMEM((2, 4 * ROWS, 256), BF16),
            pltpu.VMEM((2, 4 * ROWS, 256), BF16),
            pltpu.VMEM((CHUNKS, ROWS, CH * 16), BF16),
            pltpu.VMEM((8, 256, 4 * ROWS), BF16),
            pltpu.VMEM((8, 256, 4 * ROWS), BF16),
            pltpu.VMEM((NE, 16, 256), BF16),
            pltpu.VMEM((NE, 16, 256), BF16),
            pltpu.VMEM((NE, 16, 256), BF16),
            pltpu.VMEM((NE, 16, 256), BF16),
            pltpu.VMEM((NE, 16, 256), BF16),
            pltpu.VMEM((NE, 16, 256), BF16),
            pltpu.VMEM((NE, 16, 256), BF16),
            pltpu.VMEM((NE, 16, 256), BF16),
            pltpu.VMEM((NE, 1, 128), F32),
            pltpu.VMEM((NE, 1, 128), F32),
            pltpu.VMEM((CHUNKS, CROWS, WIDTH), BF16),
            pltpu.VMEM((CHUNKS, CROWS, WIDTH), BF16),
            pltpu.VMEM((CHUNKS, CROWS, 128), F32),
            pltpu.VMEM((CHUNKS, CROWS, 128), F32),
            pltpu.VMEM((2 * CROWS, WIDTH), BF16),
            pltpu.VMEM((2 * CROWS, WIDTH), BF16),
            pltpu.VMEM((2 * CROWS, HID), BF16),
            pltpu.VMEM((2 * CROWS, HID), BF16),
            pltpu.VMEM((WIDTH, HID), F32),
            pltpu.VMEM((HID, WIDTH), F32),
            pltpu.VMEM((4 * ROWS, 256), F32),
            dma((6,)),
            pltpu.SemaphoreType.REGULAR((2,)),
            dma((3, 2)),
            dma((3, 2)),
            dma,
            dma((CHUNKS,)),
            dma((CHUNKS,)),
            dma((2, CHUNKS)),
            dma((CHUNKS,)),
            dma((CHUNKS,)),
            dma,
            dma((CHUNKS,)),
            dma,
            dma((CHUNKS,)),
            dma((CHUNKS,)),
            dma((CHUNKS,)),
            dma((CHUNKS,)),
            dma((CHUNKS,)),
        ],
        compiler_params=pltpu.CompilerParams(
            collective_id=0, has_side_effects=True, vmem_limit_bytes=48 << 20
        ),
        name="experts",
    )(
        *(
            pltpu.with_memory_space_constraint(array, pltpu.HBM)
            for array in (routes.T, gates.T, inputs, cotangent, w_in[0], w_out[0])
        )
    )
    dx, gate, gin, gout = pl.pallas_call(
        flush,
        out_shape=tuple(jax.ShapeDtypeStruct(shape, kind) for shape, kind in shapes),
        in_specs=[vmem] * 4,
        out_specs=(hbm,) * 4,
        scratch_shapes=[dma((4,))],
        compiler_params=pltpu.CompilerParams(vmem_limit_bytes=1 << 20),
        name="flush",
    )(*outs)
    return dx, gate.T, gin[None], gout[None]


def solution(mesh):
    return jax.shard_map(
        body,
        mesh=mesh,
        in_specs=(
            P(("dp", "expert"), None),
            P(("dp", "expert"), None),
            P(("dp", "expert"), None),
            P(("dp", "expert"), None),
            P("expert", None, "dp"),
            P("expert", "dp", None),
        ),
        out_specs=(
            P(("dp", "expert"), None),
            P(("dp", "expert"), None),
            P("expert", None, "dp"),
            P("expert", "dp", None),
        ),
        check_vma=False,
    )
```

time: 96.9 us -> 84.5 us (0.87)
  local copies, waits for them, and re-layouts: 7.42 us -> 0 us
  Pallas kernels: 88.7 us -> 83.8 us
    unnamed x6 -> x0, local copies, waits for them, and re-layouts: 7.42 us -> none
    pallas_call x1 -> x2, Pallas kernels: 88.7 us -> 83.8 us  [the longest x1 81.7 us: body(): pl.pallas_call(kernel, out_shape=tuple((pltpu.VMEM(shape, kind) for shape...]
where the time goes in v2:
time: 84.5 us; the launch traced here: 84.4 us
  Pallas kernels  83.8 us (99%)
    pallas_call x1, Pallas kernels, body(): pl.pallas_call(kernel, out_shape=tuple((pltpu.VMEM(shape, kind) for shape...  81.7 us
    pallas_call x1, Pallas kernels, body(): pl.pallas_call(flush, out_shape=tuple((jax.ShapeDtypeStruct(shape, kind)...  2.12 us

profile of v2, /device:TPU:1, one launch (start us, length us, event | category | flops | bytes accessed | tf_op | source)
XLA Modules:
  0.0 84.4 jit_solution(15878917964208740922)
XLA Ops:
  0.6 81.7 %experts.1 = (bf16[32,4096]{1,0:T(8,128)(2,1)S(1)}, f32[2,128]{1,0:T(2,128)S(1)}, bf16[1024,1024]{1,0:T(8,128)(2,1)S(1)}, bf16[1024,1024]{1,0:T(8,128)(2,1)S(1)}) custom-call(s32[2,128]{1,0:T(2,128)} %bitcast.9, bf16[2,128]{1,0:T(2,128)(2,1)} %bitcast.10, bf16[32,4096]{1,0:T(8,128)(2,1)} %x_hbm.1, bf16[32,4096]{1,0:T(8,128)(2,1)} %g_hbm.1, ...), custom_call_target="tpu_custom_call" | custom-call | tf_op jit(solution)/shard_map/experts/pallas_call | solution.py:494
  82.3 2.1 %flush.1 = (bf16[32,4096]{1,0:T(8,128)(2,1)}, f32[2,128]{1,0:T(2,128)}, bf16[1024,1024]{1,0:T(8,128)(2,1)}, bf16[1024,1024]{1,0:T(8,128)(2,1)}) custom-call(bf16[32,4096]{1,0:T(8,128)(2,1)S(1)} %get-tuple-element.12.dx, f32[2,128]{1,0:T(2,128)S(1)} %get-tuple-element.13.gate, bf16[1024,1024]{1,0:T(8,128)(2,1)S(1)} %get-tuple-element.14.gin, ...), custom_call_target="tpu_custom_call" | custom-call | tf_op jit(solution)/shard_map/flush/pallas_call | solution.py:568

commit v3 on v2

--- a/solution.py
+++ b/solution.py
@@ -22,12 +22,14 @@
 CH = NE // CHUNKS
 GROUP = 16
 CROWS = CH * CAP
-SIZES = (8, 4, 4)
+OWN = 4
+HALVES = 5
 
 
 def offsets(k):
-    plane, place = k >> 4, k & 15
-    dz = (4 - (plane >> 1)) * (1 - 2 * (plane & 1)) + 4 * (1 - ((plane + 7) >> 3))
+    high, low, place = k >> 6, (k >> 5) & 1, k & 15
+    second, third, fourth = (1 - high) * low, high * (1 - low), high * low
+    dz = (1 + 2 * second - 3 * third + fourth) * (1 - 2 * ((k >> 4) & 1)) + 2 * third
     return dz, place >> 2, place & 3
 
 
@@ -171,6 +173,10 @@
         return copies
 
     hand_x = hand(1, x_hbm, near_x)
+    load_in = pltpu.make_async_copy(win_hbm, win, w_sem.at[0])
+    load_out = pltpu.make_async_copy(wout_hbm, wout, w_sem.at[1])
+    load_in.start()
+    load_out.start()
     greet(line_sem.at[0], 1)
 
     row, col = iota((ROWS, ROWS), 0), iota((ROWS, ROWS), 1)
@@ -184,7 +190,6 @@
     raw_table[2:4, :] = gates_ref[...].astype(F32)
     table[...] = dot(raw_table[...].astype(BF16), reorder)
     hand_table = hand(0, table, near_table)
-    hand_g = hand(2, g_hbm, near_g)
 
     def stack(source, target):
         for h in range(HEADS):
@@ -215,74 +220,90 @@
             plan_x[unit, at, cols] = jnp.where(part == p, hit, 0.0).astype(BF16)
             plan_s[unit, at, cols] = jnp.where(part == p, gated, 0.0).astype(BF16)
 
-    def place(unit, plans, stacks, sends, recvs, sems, side):
-        base, start, stop = unit * 16, 0, 16
-        if unit == 1:
-            start, stop = side * 8, side * 8 + 8
+    def build(unit, side, plans, stacks, sends):
+        start, stop = (side * 8, side * 8 + 8) if unit == HALVES else (0, 16)
         tokens = stacks if side is None else stacks.at[side]
-        lines = slice(start * 16, stop * 16)
-        made = dot(plans[unit, lines, :], tokens[...]).astype(BF16)
-        sends[base + start : base + stop] = made.reshape(stop - start, 16, 256)
-        lift = 0 if side is None else (-1, 1)[side]
-        sem = sems.at[unit // 2]
-        if unit in (0, 6, 7):
-            pltpu.make_async_copy(sends.at[base], recvs.at[base], sem).start()
-            start = 1
+        made = dot(plans[unit, start * 16 : stop * 16, :], tokens[...]).astype(BF16)
+        sends[unit * 16 + start : unit * 16 + stop] = made.reshape(stop - start, 16, 256)
+
+    def post(units, sends, recvs, sems):
+        for unit, side in units:
+            if unit in (0, 1, OWN):
+                k = unit * 16
+                pltpu.make_async_copy(sends.at[k], recvs.at[k], sems.at[unit // 2]).start()
 
         def push(i, carry):
-            k = base + i
-            pltpu.make_async_remote_copy(
-                sends.at[k],
-                recvs.at[k],
-                send_sem,
-                sem,
-                device_id=(dp, partner(me, k, 1, lift)),
-                device_id_type=MESH,
-            ).start()
+            for unit, side in units:
+                if unit in (0, 1, OWN):
+                    place = lax.rem(i - 1 + 4 * unit, 15) + 1
+                else:
+                    place = (i + 5 * unit) & 15
+                k = unit * 16 + place
+                lift = 0 if side is None else 2 * side - 1
+                if unit == HALVES:
+                    lift = 2 * (place >> 3) - 1
+                copy = pltpu.make_async_remote_copy(
+                    sends.at[k],
+                    recvs.at[k],
+                    send_sem,
+                    sems.at[unit // 2],
+                    device_id=(dp, partner(me, k, 1, lift)),
+                    device_id_type=MESH,
+                )
+                if unit in (0, 1, OWN):
+                    pl.when(i > 0)(copy.start)
+                else:
+                    copy.start()
             return carry
 
-        lax.fori_loop(start, stop, push, 0)
-
-    plan(0, table[...], 256, 0, me, 0)
+        lax.fori_loop(0, 16, push, 0)
+
+    plan(OWN, table[...], 256, 0, me, OWN * 16)
     loads[2].wait()
     loads[3].wait()
     stack(x_ref, stack_x)
     stack(g_ref, stack_g)
     pl.semaphore_wait(line_sem.at[1], 3)
-    place(0, plan_x, stack_x, send_x, recv_x, rx_sem, None)
-    place(0, plan_s, stack_g, send_s, recv_s, rs_sem, None)
+    for plans, stacks, sends, recvs, sems in (
+        (plan_x, stack_x, send_x, recv_x, rx_sem),
+        (plan_s, stack_g, send_s, recv_s, rs_sem),
+    ):
+        build(OWN, None, plans, stacks, sends)
+        post(((OWN, None),), sends, recvs, sems)
+    hand_g = hand(2, g_hbm, near_g)
     for side in range(2):
         hand_table[side].wait_recv()
     origins = (along(0, -1)[1], along(0, 1)[1])
-    units = ((1, 0), (1, 1), (2, 0), (3, 1), (6, 0), (7, 1), (4, 0), (5, 1))
+    units = ((2, 0), (3, 1), (0, 0), (1, 1), (6, 0), (7, 1), (HALVES, 0), (HALVES, 1))
     for unit, side in units:
-        lines, first_line = (128, 128 * side) if unit == 1 else (256, 0)
+        lines, first_line = (128, 128 * side) if unit == HALVES else (256, 0)
         plan(unit, near_table[side], lines, first_line, origins[side], unit * 16)
-    for side in range(2):
-        hand_x[side].wait_recv()
-        stack(near_x.at[side], near_stack_x.at[side])
-    for unit, side in units:
-        place(unit, plan_x, near_stack_x, send_x, recv_x, rx_sem, side)
-    for side in range(2):
-        hand_g[side].wait_recv()
-        stack(near_g.at[side], near_stack_g.at[side])
-    for unit, side in units:
-        place(unit, plan_s, near_stack_g, send_s, recv_s, rs_sem, side)
-
-    load_in = pltpu.make_async_copy(win_hbm, win, w_sem.at[0])
-    load_out = pltpu.make_async_copy(wout_hbm, wout, w_sem.at[1])
-    load_in.start()
-    load_out.start()
-
-    def remember(j, carry):
-        _, _, hit = chosen(table[...], CH * 16, 0, me, j * CH)
-        hits[j] = hit.T.astype(BF16)
-        return carry
-
-    lax.fori_loop(0, CHUNKS, remember, 0)
     gin[...] = jnp.zeros_like(gin)
     gout[...] = jnp.zeros_like(gout)
     acc[...] = jnp.zeros_like(acc)
+    kinds = (
+        (hand_x, near_x, near_stack_x, plan_x, send_x, recv_x, rx_sem),
+        (hand_g, near_g, near_stack_g, plan_s, send_s, recv_s, rs_sem),
+    )
+
+    def arrive(kind):
+        handed, raw, stacks = kinds[kind][:3]
+        for side in range(2):
+            handed[side].wait_recv()
+            stack(raw.at[side], stacks.at[side])
+
+    def relay(kind, some):
+        stacks, plans, sends, recvs, sems = kinds[kind][2:]
+        for unit, side in some:
+            build(unit, side, plans, stacks, sends)
+        post(tuple(pair for pair in some if pair != (HALVES, 1)), sends, recvs, sems)
+
+    arrive(0)
+    relay(0, units[:4])
+    arrive(1)
+    relay(1, units[:4])
+    relay(0, units[4:])
+    relay(1, units[4:])
     load_in.wait()
     load_out.wait()
 
@@ -379,13 +400,14 @@
         gather = (iota((CH, CROWS), 0) == (iota((CH, CROWS), 1) >> 2)).astype(F32)
         dsend[mine] = dot(gather, spread, precision=lax.Precision.HIGHEST).reshape(CH, 1, 128)
 
-        @pl.when(j == 0)
+        @pl.when(j == OWN // 2)
         def _():
-            pltpu.make_async_copy(back.at[0], ret.at[0], brecv_sem.at[0]).start()
-            pltpu.make_async_copy(dsend.at[0], dret.at[0], drecv_sem.at[0]).start()
+            k = OWN * 16
+            pltpu.make_async_copy(back.at[k], ret.at[k], brecv_sem.at[j]).start()
+            pltpu.make_async_copy(dsend.at[k], dret.at[k], drecv_sem.at[j]).start()
 
         def push(i, c):
-            k = j * CH + i
+            k = j * CH + (i & 1) * 16 + (i >> 1)
             target = (dp, partner(me, k, -1))
             pltpu.make_async_remote_copy(
                 back.at[k],
@@ -405,11 +427,17 @@
             ).start()
             return c
 
-        lax.fori_loop(jnp.where(j == 0, 1, 0), CH, push, 0)
+        lax.fori_loop(jnp.where(j == OWN // 2, 1, 0), CH, push, 0)
         return carry
 
     lax.fori_loop(0, CHUNKS, step, 0)
 
+    def remember(j, carry):
+        _, _, hit = chosen(table[...], CH * 16, 0, me, j * CH)
+        hits[j] = hit.T.astype(BF16)
+        return carry
+
+    lax.fori_loop(0, CHUNKS, remember, 0)
     gin_out[...] = gin[...].astype(BF16)
     gout_out[...] = gout[...].astype(BF16)
 

time: 84.5 us -> 80.7 us (0.955)
  Pallas kernels: 83.8 us -> 80 us
    pallas_call x1, Pallas kernels: 81.7 us -> 77.9 us  [body(): pl.pallas_call(kernel, out_shape=tuple((pltpu.VMEM(shape, kind) for shape...]
where the time goes in v3:
time: 80.7 us
  Pallas kernels  80 us (99%)
    pallas_call x1, Pallas kernels, body(): pl.pallas_call(kernel, out_shape=tuple((pltpu.VMEM(shape, kind) for shape...  77.9 us
    pallas_call x1, Pallas kernels, body(): pl.pallas_call(flush, out_shape=tuple((jax.ShapeDtypeStruct(shape, kind)...  2.12 us

profile of v3, /device:TPU:1, one launch (start us, length us, event | category | flops | bytes accessed | tf_op | source)
XLA Modules:
  0.0 80.7 jit_solution(8083575614608153931)
XLA Ops:
  0.6 77.9 %experts.1 = (bf16[32,4096]{1,0:T(8,128)(2,1)S(1)}, f32[2,128]{1,0:T(2,128)S(1)}, bf16[1024,1024]{1,0:T(8,128)(2,1)S(1)}, bf16[1024,1024]{1,0:T(8,128)(2,1)S(1)}) custom-call(s32[2,128]{1,0:T(2,128)} %bitcast.9, bf16[2,128]{1,0:T(2,128)(2,1)} %bitcast.10, bf16[32,4096]{1,0:T(8,128)(2,1)} %x_hbm.1, bf16[32,4096]{1,0:T(8,128)(2,1)} %g_hbm.1, ...), custom_call_target="tpu_custom_call" | custom-call | tf_op jit(solution)/shard_map/experts/pallas_call | solution.py:522
  78.5 2.1 %flush.1 = (bf16[32,4096]{1,0:T(8,128)(2,1)}, f32[2,128]{1,0:T(2,128)}, bf16[1024,1024]{1,0:T(8,128)(2,1)}, bf16[1024,1024]{1,0:T(8,128)(2,1)}) custom-call(bf16[32,4096]{1,0:T(8,128)(2,1)S(1)} %get-tuple-element.12.dx, f32[2,128]{1,0:T(2,128)S(1)} %get-tuple-element.13.gate, bf16[1024,1024]{1,0:T(8,128)(2,1)S(1)} %get-tuple-element.14.gin, ...), custom_call_target="tpu_custom_call" | custom-call | tf_op jit(solution)/shard_map/flush/pallas_call | solution.py:596

commit v4 on v3

--- a/solution.py
+++ b/solution.py
@@ -235,9 +235,9 @@
         def push(i, carry):
             for unit, side in units:
                 if unit in (0, 1, OWN):
-                    place = lax.rem(i - 1 + 4 * unit, 15) + 1
+                    place = lax.rem(i + 14 + 4 * unit + 7 * dp, 15) + 1
                 else:
-                    place = (i + 5 * unit) & 15
+                    place = (i + 5 * unit + 8 * dp) & 15
                 k = unit * 16 + place
                 lift = 0 if side is None else 2 * side - 1
                 if unit == HALVES:
@@ -407,27 +407,24 @@
             pltpu.make_async_copy(dsend.at[k], dret.at[k], drecv_sem.at[j]).start()
 
         def push(i, c):
-            k = j * CH + (i & 1) * 16 + (i >> 1)
+            k = j * CH + (i & 1) * 16 + (((i >> 1) + 8 * dp) & 15)
             target = (dp, partner(me, k, -1))
-            pltpu.make_async_remote_copy(
-                back.at[k],
-                ret.at[k],
-                bsend_sem,
-                brecv_sem.at[j],
-                device_id=target,
-                device_id_type=MESH,
-            ).start()
-            pltpu.make_async_remote_copy(
-                dsend.at[k],
-                dret.at[k],
-                dsend_sem,
-                drecv_sem.at[j],
-                device_id=target,
-                device_id_type=MESH,
-            ).start()
+            for source, place, left, came in (
+                (back, ret, bsend_sem, brecv_sem),
+                (dsend, dret, dsend_sem, drecv_sem),
+            ):
+                copy = pltpu.make_async_remote_copy(
+                    source.at[k],
+                    place.at[k],
+                    left,
+                    came.at[j],
+                    device_id=target,
+                    device_id_type=MESH,
+                )
+                pl.when(k != OWN * 16)(copy.start)
             return c
 
-        lax.fori_loop(jnp.where(j == OWN // 2, 1, 0), CH, push, 0)
+        lax.fori_loop(0, CH, push, 0)
         return carry
 
     lax.fori_loop(0, CHUNKS, step, 0)

time: 80.7 us -> 79.1 us (0.980)
  Pallas kernels: 80 us -> 78.4 us
    pallas_call x1, Pallas kernels: 77.9 us -> 76.3 us  [body(): pl.pallas_call(kernel, out_shape=tuple((pltpu.VMEM(shape, kind) for shape...]
where the time goes in v4:
time: 79.1 us; the launch traced here: 79 us
  Pallas kernels  78.4 us (99%)
    pallas_call x1, Pallas kernels, body(): pl.pallas_call(kernel, out_shape=tuple((pltpu.VMEM(shape, kind) for shape...  76.3 us
    pallas_call x1, Pallas kernels, body(): pl.pallas_call(flush, out_shape=tuple((jax.ShapeDtypeStruct(shape, kind)...  2.12 us

profile of v4, /device:TPU:1, one launch (start us, length us, event | category | flops | bytes accessed | tf_op | source)
XLA Modules:
  0.0 79.0 jit_solution(1530601418399939514)
XLA Ops:
  0.6 76.3 %experts.1 = (bf16[32,4096]{1,0:T(8,128)(2,1)S(1)}, f32[2,128]{1,0:T(2,128)S(1)}, bf16[1024,1024]{1,0:T(8,128)(2,1)S(1)}, bf16[1024,1024]{1,0:T(8,128)(2,1)S(1)}) custom-call(s32[2,128]{1,0:T(2,128)} %bitcast.9, bf16[2,128]{1,0:T(2,128)(2,1)} %bitcast.10, bf16[32,4096]{1,0:T(8,128)(2,1)} %x_hbm.1, bf16[32,4096]{1,0:T(8,128)(2,1)} %g_hbm.1, ...), custom_call_target="tpu_custom_call" | custom-call | tf_op jit(solution)/shard_map/experts/pallas_call | solution.py:519
  76.9 2.1 %flush.1 = (bf16[32,4096]{1,0:T(8,128)(2,1)}, f32[2,128]{1,0:T(2,128)}, bf16[1024,1024]{1,0:T(8,128)(2,1)}, bf16[1024,1024]{1,0:T(8,128)(2,1)}) custom-call(bf16[32,4096]{1,0:T(8,128)(2,1)S(1)} %get-tuple-element.12.dx, f32[2,128]{1,0:T(2,128)S(1)} %get-tuple-element.13.gate, bf16[1024,1024]{1,0:T(8,128)(2,1)S(1)} %get-tuple-element.14.gin, ...), custom_call_target="tpu_custom_call" | custom-call | tf_op jit(solution)/shard_map/flush/pallas_call | solution.py:593
